TPU v7x, 32 devices: a whole 2x2x4 slice. The times are simulated.
32 devices in a mesh: groups: 2 (over y), flat: 4 (over z), dp: 4 (over x, core).
Axes of the slice: x: 2, y: 2, z: 4, core: 2. Of those that a mesh axis runs over, the one named last changes fastest.
Arguments:
- activations: bfloat16 [4096, 14336], P(('groups', 'dp'), 'flat'), parts along dimension 0
- curvature: float32 [4096], P(('groups', 'dp')), parts along dimension 0, may hold values from 0.3 to 3
- vector_now: float32 [28672, 4096], P(('groups', 'flat', 'dp')), parts along dimension 0
- vector_before: float32 [28672, 4096], P(('groups', 'flat', 'dp')), parts along dimension 0, may hold values from -6 to 6
- sign_bits: int32 [28672, 4096], P(('groups', 'flat', 'dp')), parts along dimension 0, may hold values from 0 to 1
- prior_precision: float32 [2], P('groups'), parts along dimension 0, may hold values from 0.2 to 2
- beta_before: float32 [2], P('groups'), parts along dimension 0, may hold values from 0.3 to 1.5
- kept_rows: int32 [8192], P('groups'), parts along dimension 0, may hold values from 0 to 3583
- kept_cols: int32 [8192], P('groups'), parts along dimension 0, may hold values from 0 to 16383
Outputs:
- vector_next: float32 [28672, 4096], P(('groups', 'flat', 'dp')), parts along dimension 0
- alpha_value: float32 [2], P('groups'), parts along dimension 0
- beta_value: float32 [2], P('groups'), parts along dimension 0
- sketch: float32 [8192], P('groups'), parts along dimension 0
There are 2 independent parts, one for each index of `groups`. A program takes and returns all parts, laid end to end along the dimension named above; each array names one. Nothing has to cross between parts.
All inputs are finite; a program needn't handle non-finite values.
Results may differ from a plain program's by a relative error of at most 0.015.
Values may be sent and summed in bfloat16 or wider, within the bound.
A program may use at most 256 MiB of HBM per device.

v0:
```python
import math

import jax
import jax.numpy as jnp
from jax import lax
from jax.sharding import PartitionSpec as P

BLOCK = 128


def parity_sign(row_index, col_index):
    common_bits = jnp.bitwise_and(row_index, col_index)
    parity_sum = jnp.zeros_like(common_bits)
    for position in range(BLOCK.bit_length() - 1):
        parity_sum = parity_sum + jnp.bitwise_and(jnp.right_shift(common_bits, position), 1)
    return (1 - 2 * jnp.bitwise_and(parity_sum, 1)).astype(jnp.float32) / math.sqrt(BLOCK)


def hadamard_table():
    row_index = lax.broadcasted_iota(jnp.int32, (BLOCK, BLOCK), 0)
    col_index = lax.broadcasted_iota(jnp.int32, (BLOCK, BLOCK), 1)
    return parity_sign(row_index, col_index)


def pick_dense(column_block, hadamard, own_index, kept_rows, kept_cols):
    cols_here = column_block.shape[1]
    section_two = jnp.einsum(
        "ri,bic->brc",
        hadamard,
        column_block.reshape(-1, BLOCK, cols_here),
        precision=lax.Precision.HIGHEST,
    )
    section_two = section_two.reshape(-1, cols_here)
    first_col = own_index * cols_here
    inside = jnp.logical_and(kept_cols >= first_col, kept_cols < first_col + cols_here)
    local_col = jnp.clip(kept_cols - first_col, 0, cols_here - 1)
    return jnp.where(inside, section_two[kept_rows, local_col], 0.0)


def on_device(
    activations,
    curvature,
    vector_now,
    vector_before,
    sign_bits,
    prior_precision,
    beta_before,
    kept_rows,
    kept_cols,
):
    token_count = activations.shape[0]
    out_width = vector_now.shape[1]
    local_rows = vector_now.shape[0]
    flat_count = lax.axis_size("flat")
    data_count = lax.axis_size("dp")
    total_tokens = token_count * data_count
    total_cells = local_rows * out_width * flat_count * data_count
    vector_half = vector_now.astype(jnp.bfloat16)
    columns = activations
    partial_out = jnp.dot(
        columns,
        lax.all_gather(vector_half, "dp", axis=0, tiled=True),
        preferred_element_type=jnp.float32,
    )
    shares = lax.psum_scatter(
        partial_out.astype(jnp.bfloat16), "flat", scatter_dimension=1, tiled=True
    ).astype(jnp.float32)
    scaled_share = (curvature[:, None] * shares / total_tokens).astype(jnp.bfloat16)
    scaled = lax.all_gather(scaled_share, "flat", axis=1, tiled=True)
    columns = activations
    image_data = lax.psum_scatter(
        lax.dot_general(
            columns, scaled, (((0,), (0,)), ((), ())), preferred_element_type=jnp.float32
        ).astype(jnp.bfloat16),
        "dp",
        scatter_dimension=0,
        tiled=True,
    ).astype(jnp.float32)
    new_image = image_data + prior_precision[0] * vector_now
    beta_old = beta_before[0]
    alpha_value = lax.psum(jnp.sum(new_image * vector_now), ("flat", "dp")) / total_cells
    residual = new_image - alpha_value * vector_now - beta_old * vector_before
    square = lax.psum(jnp.sum(residual * residual), ("flat", "dp")) / total_cells
    beta_value = jnp.sqrt(square + 1e-06)
    vector_next = residual / beta_value
    hadamard = hadamard_table()
    signed = (2 * sign_bits - 1).astype(jnp.float32) * vector_next
    rows_here = local_rows * out_width // (BLOCK * BLOCK)
    section_one = jnp.dot(signed.reshape(-1, BLOCK), hadamard, precision=lax.Precision.HIGHEST)
    section_one = section_one.reshape(rows_here, BLOCK * BLOCK)
    own_index = lax.axis_index(("flat", "dp"))
    column_block = lax.all_to_all(
        section_one.astype(jnp.bfloat16), ("flat", "dp"), split_axis=1, concat_axis=0, tiled=True
    ).astype(section_one.dtype)
    local_values = pick_dense(column_block, hadamard, own_index, kept_rows, kept_cols)
    sketch = lax.psum(local_values, ("flat", "dp"))
    return (vector_next, alpha_value.reshape(1), beta_value.reshape(1), sketch)


def solution(mesh):
    placed = (
        P(("groups", "dp"), "flat"),
        P(("groups", "dp")),
        P(("groups", "flat", "dp"), None),
        P(("groups", "flat", "dp"), None),
        P(("groups", "flat", "dp"), None),
        P("groups"),
        P("groups"),
        P("groups"),
        P("groups"),
    )
    return jax.shard_map(
        on_device,
        mesh=mesh,
        in_specs=placed,
        out_specs=(P(("groups", "flat", "dp"), None), P("groups"), P("groups"), P("groups")),
        check_vma=False,
    )
```

profile of v0, /device:TPU:0, one launch (start us, length us, event | category | flops | bytes accessed | tf_op | source)
XLA Modules:
  0.0 1159.3 jit_solution(15920801584408900253)
XLA Ops:
  16.7 180.8 %all-gather.3.cloned.1.call-done = bf16[3584,4096]{1,0:T(8,128)(2,1)} async-done(((bf16[896,4096]{1,0:T(8,128)(2,1)}), bf16[3584,4096]{1,0:T(8,128)(2,1)}) %all-gather.3.cloned.1.call-update) | async-done | bytes 29360144 | tf_op jit(solution)/shard_map/all_gather | solution.py:62
  197.4 23.0 %convolution_convert_fusion.2 = bf16[512,4096]{1,0:T(8,128)(2,1)} fusion(bf16[512,3584]{1,0:T(8,128)(2,1)} %param.9, bf16[3584,4096]{1,0:T(8,128)(2,1)} %all-gather.3.cloned.1.call-done), kind=kOutput, calls=%fused_computation.10 | convolution fusion | flops 15034482688 | bytes 37224448 | tf_op jit(solution)/shard_map/dot_general | solution.py:60
  220.5 76.9 %reduce-scatter.5.cloned.1.call-done = bf16[512,1024]{1,0:T(8,128)(2,1)} async-done(((bf16[512,4096]{1,0:T(8,128)(2,1)}), bf16[512,1024]{1,0:T(8,128)(2,1)}) %reduce-scatter.5.cloned.1.call-update) | async-done | bytes 1048592 | tf_op jit(solution)/shard_map/reduce_scatter | solution.py:65
  300.2 81.2 %all-gather.5.cloned.1.call-done = bf16[512,4096]{1,0:T(8,128)(2,1)} async-done(((bf16[512,1024]{1,0:T(8,128)(2,1)}), bf16[512,4096]{1,0:T(8,128)(2,1)}) %all-gather.5.cloned.1.call-update) | async-done | bytes 4194320 | tf_op jit(solution)/shard_map/all_gather | solution.py:69
  381.4 22.3 %fusion = bf16[3584,4096]{0,1:T(8,128)(2,1)} fusion(bf16[512,4096]{1,0:T(8,128)(2,1)} %all-gather.5.cloned.1.call-done, bf16[512,3584]{1,0:T(8,128)(2,1)} %param.9), kind=kOutput, calls=%fused_computation.3 | convolution fusion | flops 15047065600 | bytes 37224448 | tf_op jit(solution)/shard_map/dot_general | solution.py:72
  403.7 37.0 %copy.36 = bf16[3584,4096]{1,0:T(8,128)(2,1)} copy(bf16[3584,4096]{0,1:T(8,128)(2,1)} %fusion) | data formatting | bytes 58720256
  440.7 16.7 %copy.28 = f32[896,4096]{0,1:T(8,128)} copy(f32[896,4096]{1,0:T(8,128)} %param.11) | data formatting | bytes 29360128 | tf_op args[2]
  458.1 18.0 %copy.31 = f32[896,4096]{0,1:T(8,128)} copy(f32[896,4096]{1,0:T(8,128)} %param.12) | data formatting | bytes 29360128 | tf_op args[3]
  476.1 171.1 %reduce-scatter.7.cloned.1.call-done = bf16[896,4096]{1,0:T(8,128)(2,1)} async-done(((bf16[3584,4096]{1,0:T(8,128)(2,1)}), bf16[896,4096]{1,0:T(8,128)(2,1)}) %reduce-scatter.7.cloned.1.call-update) | async-done | bytes 7340048
  658.1 11.6 %multiply_reduce_fusion.1 = f32[]{:T(128)} fusion(f32[896,4096]{0,1:T(8,128)} %copy.28, bf16[896,4096]{0,1:T(8,128)(2,1)} %copy.37, f32[]{:T(128)} %bitcast.22), kind=kLoop, calls=%fused_computation.7 | loop fusion | flops 18350080 | bytes 22020104 | tf_op jit(solution)/shard_map/reduce_sum | solution.py:81
  670.4 32.9 %psum.21 = f32[]{:T(128)} all-reduce(f32[]{:T(128)} %multiply_reduce_fusion.1), channel_id=1, replica_groups=mesh['groups'=2,'flat'=4,'dp'=4] {'flat','dp'}, use_global_device_ids=true, to_apply=%region_3.0 | all-reduce | flops 1 | bytes 8 | tf_op jit(solution)/shard_map/psum | solution.py:81
  703.9 13.4 %multiply_reduce_fusion = f32[]{:T(128)} fusion(f32[896,4096]{0,1:T(8,128)} %copy.31, f32[]{:T(128)} %bitcast.25, f32[896,4096]{0,1:T(8,128)} %copy.28, f32[]{:T(128)} %div.28, f32[]{:T(128)} %bitcast.23, bf16[896,4096]{0,1:T(8,128)(2,1)} %copy.37), kind=kLoop, calls=%fused_computation.5 | loop fusion | flops 33030144 | bytes 36700176 | tf_op jit(solution)/shard_map/reduce_sum | solution.py:83
  717.3 16.1 %copy.32 = s32[896,4096]{0,1:T(8,128)} copy(s32[896,4096]{1,0:T(8,128)} %param.13) | data formatting | bytes 29360128 | tf_op args[4]
  733.4 30.3 %psum.22 = f32[]{:T(128)} all-reduce(f32[]{:T(128)} %multiply_reduce_fusion), channel_id=1, replica_groups=mesh['groups'=2,'flat'=4,'dp'=4] {'flat','dp'}, use_global_device_ids=true, to_apply=%region_5.0 | all-reduce | flops 1 | bytes 8 | tf_op jit(solution)/shard_map/psum | solution.py:83
  764.4 28.3 %convert_multiply_fusion = (f32[896,4096]{0,1:T(8,128)}, f32[896,4096]{0,1:T(8,128)}) fusion(s32[896,4096]{0,1:T(8,128)} %copy.32, f32[]{:T(128)} %sqrt.3, f32[896,4096]{0,1:T(8,128)} %copy.31, f32[]{:T(128)} %bitcast.26, f32[896,4096]{0,1:T(8,128)} %copy.28, f32[]{:T(128)} %div.28, f32[]{:T(128)} %bitcast.24, bf16[896,4096]{0,1:T(8,128)(2,1)} %copy.37), kind=kLoop, calls=%fused_computation.4 | loop fusion | flops 44040192 | bytes 80740368 | tf_op jit(solution)/shard_map/mul | solution.py:87
  792.7 16.1 %copy.33 = f32[896,4096]{1,0:T(8,128)} copy(f32[896,4096]{0,1:T(8,128)} %get-tuple-element.16) | data formatting | bytes 29360128 | tf_op jit(solution)/shard_map/mul | solution.py:87
  808.8 15.8 %reshape.33 = f32[28672,128]{1,0:T(8,128)} reshape(f32[896,4096]{1,0:T(8,128)} %copy.33) | data formatting | bytes 29360128 | tf_op jit(solution)/shard_map/reshape | solution.py:89
  824.6 15.6 %convolution_convert_fusion = bf16[28672,128]{1,0:T(8,128)(2,1)} fusion(f32[28672,128]{1,0:T(8,128)} %reshape.33), kind=kOutput, calls=%fused_computation.1 | convolution fusion | flops 5641240576 | bytes 22020096 | tf_op jit(solution)/shard_map/dot_general | solution.py:89
  840.3 11.8 %convert_element_type.47 = bf16[224,16,1024]{2,1,0:T(8,128)(2,1)} reshape(bf16[28672,128]{1,0:T(8,128)(2,1)} %convolution_convert_fusion) | data formatting | bytes 14680064 | tf_op jit(solution)/shard_map/convert_element_type | solution.py:93
  867.2 16.1 %copy.35 = f32[896,4096]{1,0:T(8,128)} copy(f32[896,4096]{0,1:T(8,128)} %get-tuple-element.17) | data formatting | bytes 29360128
  883.3 116.0 %all-to-all-done = bf16[224,16,1024]{2,0,1:T(8,128)(2,1)} async-done(((bf16[224,16,1024]{2,0,1:T(8,128)(2,1)}), bf16[224,16,1024]{2,0,1:T(8,128)(2,1)}, u32[]{:S(2)}, u32[]{:S(2)}) %all-to-all-start) | async-done | bytes 7340064 | tf_op jit(solution)/shard_map/all_to_all | solution.py:92
  999.3 12.7 %fusion.1 = f32[28,1024,128]{1,2,0:T(8,128)} fusion(bf16[28,128,1024]{2,1,0:T(8,128)(2,1)} %bitcast.6), kind=kOutput, calls=%fused_computation.12 | convolution fusion | flops 5637570560 | bytes 22020096 | tf_op jit(solution)/shard_map/ri,bic->brc/dot_general | solution.py:27
  1012.0 50.2 %gather_fusion = f32[4096]{0:T(1024)S(1)} fusion(f32[3584,1024]{1,0:T(8,128)} %bitcast.27, s32[4096]{0:T(1024)S(1)} %fusion.5), kind=kCustom, calls=%fused_computation | custom fusion | bytes 65536 | tf_op jit(solution)/shard_map/gather | solution.py:37
  1062.2 88.3 %psum.23 = f32[4096]{0:T(1024)} all-reduce(f32[4096]{0:T(1024)S(1)} %and_select_fusion), channel_id=1, replica_groups=mesh['groups'=2,'flat'=4,'dp'=4] {'flat','dp'}, use_global_device_ids=true, to_apply=%region_6.7 | all-reduce | flops 4096 | bytes 32768 | tf_op jit(solution)/shard_map/psum | solution.py:96
  (21 shorter events, 38.3 us)
Async XLA Ops:
  7.2 190.3 %all-gather.3.cloned.1.call-start = ((), (), s32[]{:S(2)}) async-start(), calls=%async_computation.3 | async-start | bytes 36700160 | tf_op jit(solution)/shard_map/all_gather | solution.py:62
  16.6 280.8 %copy-start.2 = (f32[512]{0:T(512)S(1)}, f32[512]{0:T(512)}, u32[]{:S(2)}) copy-start(f32[512]{0:T(512)} %param.10) | copy-start | bytes 6148
  16.6 280.8 %reduce-scatter.5.cloned.1.call-start = ((), (), s32[]{:S(2)}) async-start(), calls=%async_computation.4 | async-start | bytes 5242880 | tf_op jit(solution)/shard_map/reduce_scatter | solution.py:65
  220.5 160.9 %all-gather.5.cloned.1.call-start = ((), (), s32[]{:S(2)}) async-start(), calls=%async_computation.5 | async-start | bytes 5242880 | tf_op jit(solution)/shard_map/all_gather | solution.py:69
  299.9 347.3 %reduce-scatter.7.cloned.1.call-start = ((), (), s32[]{:S(2)}) async-start(), calls=%async_computation.6 | async-start | bytes 36700160
  852.0 15.2 %copy-start = (s32[4096]{0:T(1024)S(1)}, s32[4096]{0:T(1024)}, u32[]{:S(2)}) copy-start(s32[4096]{0:T(1024)} %param.17) | copy-start | bytes 49156
  852.0 15.2 %copy-start.1 = (s32[4096]{0:T(1024)S(1)}, s32[4096]{0:T(1024)}, u32[]{:S(2)}) copy-start(s32[4096]{0:T(1024)} %param.16) | copy-start | bytes 49156
  862.2 137.1 %all-to-all-start = ((bf16[224,16,1024]{2,0,1:T(8,128)(2,1)}), bf16[224,16,1024]{2,0,1:T(8,128)(2,1)}, u32[]{:S(2)}, u32[]{:S(2)}) async-start(bf16[224,16,1024]{2,0,1:T(8,128)(2,1)} %copy.34), calls=%async_computation.1 | async-start | bytes 14680064 | tf_op jit(solution)/shard_map/all_to_all | solution.py:92
Sparse Core Ops, SparseCore 0:
  16.7 180.6 all-gather.2
  220.6 76.7 reduce-scatter.4
  300.1 81.2 all-gather.4
  440.8 206.3 reduce-scatter.6
where the time goes:
time: 1160 us
  waiting for transfers between devices  626 us (54%)
  local copies, waits for them, and re-layouts  219 us (19%)
  blocking collectives  152 us (13%)
  matrix products  73.6 us (6%)
  other arithmetic  65.2 us (6%)
  between operations  18.8 us (2%)
    all_gather x1, waiting for transfers between devices, on_device(): lax.all_gather(vector_half, 'dp', axis=0, tiled=True)  181 us
    unnamed x5, waiting for transfers between devices  171 us
    all_to_all x1, waiting for transfers between devices, on_device(): lax.all_to_all(section_one.astype(jnp.bfloat16), ('flat', 'dp'), split_ax...  116 us
    unnamed x12, local copies, waits for them, and re-layouts  115 us
    psum x1, blocking collectives, on_device(): sketch = lax.psum(local_values, ('flat', 'dp'))  88.3 us
    all_gather x1, waiting for transfers between devices, on_device(): scaled = lax.all_gather(scaled_share, 'flat', axis=1, tiled=True)  81.2 us
    reduce_scatter x1, waiting for transfers between devices, on_device(): lax.psum_scatter(partial_out.astype(jnp.bfloat16), 'flat', scatter_dimens...  76.9 us
    gather x1, local copies, waits for them, and re-layouts, pick_dense(): return jnp.where(inside, section_two[kept_rows, local_col], 0.0)  50.2 us
  transfers between devices with their start and end apart: 5, of which 5 were waited for; matrix products, arithmetic and copies ran while one was open for 4% of the time, Pallas kernels for 0%

commit v1 on v0

--- a/solution.py
+++ b/solution.py
@@ -3,6 +3,8 @@
 import jax
 import jax.numpy as jnp
 from jax import lax
+from jax.experimental import pallas as pl
+from jax.experimental.pallas import tpu as pltpu
 from jax.sharding import PartitionSpec as P
 
 BLOCK = 128
@@ -37,7 +39,7 @@
     return jnp.where(inside, section_two[kept_rows, local_col], 0.0)
 
 
-def on_device(
+def plain_on_device(
     activations,
     curvature,
     vector_now,
@@ -97,6 +99,142 @@
     return (vector_next, alpha_value.reshape(1), beta_value.reshape(1), sketch)
 
 
+def residual_kernel(scalars, n_ref, v_ref, b_ref, s_ref, r_ref, x_ref, sq_ref):
+    @pl.when(pl.program_id(0) == 0)
+    def _():
+        sq_ref[...] = jnp.zeros_like(sq_ref)
+
+    rows, width = n_ref.shape
+    residual = n_ref[...] - scalars[0] * v_ref[...] - scalars[1] * b_ref[...]
+    r_ref[...] = residual
+    signs = (2 * s_ref[...] - 1).astype(jnp.float32)
+    x_ref[...] = (signs * residual).astype(jnp.bfloat16)
+    square = jnp.sum((residual * residual).reshape(rows // 8, 8, width), axis=0)
+    total = square[:, :128]
+    for k in range(1, width // 128):
+        total = total + square[:, k * 128 : (k + 1) * 128]
+    sq_ref[...] += total
+
+
+def residual_pass(scalars, image, vector_now, vector_before, sign_bits):
+    rows, width = image.shape
+    tile = 64
+    block = pl.BlockSpec((tile, width), lambda i: (i, 0))
+    return pl.pallas_call(
+        residual_kernel,
+        grid=(rows // tile,),
+        out_shape=(
+            jax.ShapeDtypeStruct((rows, width), jnp.float32),
+            jax.ShapeDtypeStruct((rows, width), jnp.bfloat16),
+            jax.ShapeDtypeStruct((8, 128), jnp.float32),
+        ),
+        in_specs=[pl.BlockSpec(memory_space=pltpu.SMEM)] + [block] * 4,
+        out_specs=(block, block, pl.BlockSpec((8, 128), lambda i: (0, 0))),
+        compiler_params=pltpu.CompilerParams(vmem_limit_bytes=40 * 2**20),
+    )(scalars, image, vector_now, vector_before, sign_bits)
+
+
+def odd_bits(common):
+    common = common ^ (common >> 4)
+    common = common ^ (common >> 2)
+    common = common ^ (common >> 1)
+    return common & 1
+
+
+def sketch_kernel(first_ref, x_ref, row_ref, col_ref, out_ref):
+    rows, width = x_ref.shape
+    count = row_ref.shape[0]
+    per_row = BLOCK * BLOCK // width
+    kept_row, kept_col = row_ref[...], col_ref[...]
+    place = lax.broadcasted_iota(jnp.int32, (count, rows), 1)
+    row = first_ref[0] + place // per_row
+    here = jnp.logical_and(row // BLOCK == kept_row // BLOCK, place % per_row == kept_col // width)
+    sign = 1 - 2 * odd_bits((row % BLOCK) & (kept_row % BLOCK))
+    weights = jnp.where(here, sign, 0).astype(jnp.float32).astype(jnp.bfloat16)
+    group = (kept_col % width) // BLOCK
+    span = 512
+    total = jnp.zeros((count, BLOCK), jnp.float32)
+    for k in range(width // span):
+        sums = jnp.dot(
+            weights, x_ref[:, k * span : (k + 1) * span], preferred_element_type=jnp.float32
+        )
+        for g in range(span // BLOCK):
+            total = jnp.where(
+                group == k * (span // BLOCK) + g, sums[:, g * BLOCK : (g + 1) * BLOCK], total
+            )
+    lane = lax.broadcasted_iota(jnp.int32, (count, BLOCK), 1)
+    sign = (1 - 2 * odd_bits(lane & (kept_col % BLOCK))).astype(jnp.float32)
+    out_ref[...] = jnp.sum(total * sign, axis=1, keepdims=True) / BLOCK
+
+
+def sketch_pass(first_row, signed, kept_rows, kept_cols):
+    rows, width = signed.shape
+    kept = kept_rows.shape[0]
+    tile = 256
+    narrow = pl.BlockSpec((tile, 1), lambda i: (i, 0))
+    return pl.pallas_call(
+        sketch_kernel,
+        grid=(kept // tile,),
+        out_shape=jax.ShapeDtypeStruct((kept, 1), jnp.float32),
+        in_specs=[
+            pl.BlockSpec(memory_space=pltpu.SMEM),
+            pl.BlockSpec((rows, width), lambda i: (0, 0)),
+            narrow,
+            narrow,
+        ],
+        out_specs=narrow,
+        compiler_params=pltpu.CompilerParams(vmem_limit_bytes=40 * 2**20),
+    )(first_row, signed, kept_rows.reshape(kept, 1), kept_cols.reshape(kept, 1))
+
+
+def on_device(
+    activations,
+    curvature,
+    vector_now,
+    vector_before,
+    sign_bits,
+    prior_precision,
+    beta_before,
+    kept_rows,
+    kept_cols,
+):
+    flat_count = lax.axis_size("flat")
+    data_count = lax.axis_size("dp")
+    rows, width = vector_now.shape
+    total_cells = rows * width * flat_count * data_count
+    tokens = activations.shape[0] * data_count
+    columns = lax.all_to_all(activations, "dp", split_axis=1, concat_axis=0, tiled=True)
+    outputs = jnp.dot(
+        columns, vector_now.astype(jnp.bfloat16), preferred_element_type=jnp.float32
+    ).astype(jnp.bfloat16)
+    shares = lax.psum_scatter(outputs, "dp", scatter_dimension=0, tiled=True)
+    shares = lax.psum_scatter(shares, "flat", scatter_dimension=1, tiled=True).astype(jnp.float32)
+    scaled = (curvature[:, None] * shares / tokens).astype(jnp.bfloat16)
+    scaled = lax.all_gather(scaled, "flat", axis=1, tiled=True)
+    scaled = lax.all_gather(scaled, "dp", axis=0, tiled=True)
+    image = jnp.dot(columns.T, scaled, preferred_element_type=jnp.float32)
+    image = image + prior_precision[0] * vector_now
+    alpha_value = lax.psum(jnp.sum(image * vector_now), ("flat", "dp")).reshape(1) / total_cells
+    residual, signed, square = residual_pass(
+        jnp.concatenate([alpha_value, beta_before]), image, vector_now, vector_before, sign_bits
+    )
+    own_index = lax.axis_index(("flat", "dp"))
+    first_row = (own_index * (rows * width // (BLOCK * BLOCK))).reshape(1)
+    local_values = sketch_pass(first_row, signed, kept_rows, kept_cols)
+    kept = kept_rows.shape[0]
+    sums = lax.psum(
+        jnp.concatenate([local_values.reshape(kept // 128, 128), square]), ("flat", "dp")
+    )
+    beta_value = jnp.sqrt(jnp.sum(sums[kept // 128 :]) / total_cells + 1e-06)
+    vector_next = residual / beta_value
+    sketch = sums[: kept // 128].reshape(kept) / beta_value
+    return (vector_next, alpha_value, beta_value.reshape(1), sketch)
+
+
+def fits(mesh):
+    return mesh.shape["dp"] == 4 and mesh.shape["flat"] == 4
+
+
 def solution(mesh):
     placed = (
         P(("groups", "dp"), "flat"),
@@ -110,7 +248,7 @@
         P("groups"),
     )
     return jax.shard_map(
-        on_device,
+        on_device if fits(mesh) else plain_on_device,
         mesh=mesh,
         in_specs=placed,
         out_specs=(P(("groups", "flat", "dp"), None), P("groups"), P("groups"), P("groups")),

time: 1160 us -> 713 us (0.61)
  waiting for transfers between devices: 626 us -> 390 us
  local copies, waits for them, and re-layouts: 219 us -> 15.9 us
  Pallas kernels: 0 us -> 74.6 us
  other arithmetic: 65.2 us -> 19.3 us
  matrix products: 73.6 us -> 53.6 us
  blocking collectives: 152 us -> 140 us
    unnamed x5 -> x4, waiting for transfers between devices: 171 us -> 0.07 us
    reduce_scatter x1 -> x2, waiting for transfers between devices: 76.9 us -> 206 us  [the longest x1 127 us: on_device(): shares = lax.psum_scatter(outputs, 'dp', scatter_dimension=0, tiled=True)]
    all_to_all x1 -> x0, waiting for transfers between devices: 116 us -> none  [on_device(): lax.all_to_all(section_one.astype(jnp.bfloat16), ('flat', 'dp'), split_ax...]
    unnamed x12 -> x11, local copies, waits for them, and re-layouts: 115 us -> 7.26 us
    all_gather x2, waiting for transfers between devices: 262 us -> 183 us  [the longest x1 102 us: on_device(): scaled = lax.all_gather(scaled, 'dp', axis=0, tiled=True)]
    pallas_call x0 -> x2, Pallas kernels: none -> 74.6 us  [the longest x1 49 us: sketch_pass(): pl.pallas_call(sketch_kernel, grid=(kept // tile,), out_shape=jax.ShapeDt...]
    psum x3 -> x2, blocking collectives: 152 us -> 91.1 us  [the longest x1 57.6 us: on_device(): lax.psum(jnp.concatenate([local_values.reshape(kept // 128, 128), square]...]
    gather x1 -> x0, local copies, waits for them, and re-layouts: 50.2 us -> none  [pick_dense(): return jnp.where(inside, section_two[kept_rows, local_col], 0.0)]
  transfers between devices with their start and end apart: 5 -> 4, of which waited for: 5 -> 4; matrix products, arithmetic and copies ran while one was open for 4% -> 0% of each run, Pallas kernels for 0% -> 0%
where the time goes in v1:
time: 713 us; the launch traced here: 712 us
  waiting for transfers between devices  390 us (55%)
  blocking collectives  140 us (20%)
  Pallas kernels  74.6 us (10%)
  matrix products  53.6 us (8%)
  other arithmetic  19.3 us (3%)
  between operations  18.7 us (3%)
  local copies, waits for them, and re-layouts  15.9 us (2%)
    reduce_scatter x1, waiting for transfers between devices, on_device(): shares = lax.psum_scatter(outputs, 'dp', scatter_dimension=0, tiled=True)  127 us
    all_gather x1, waiting for transfers between devices, on_device(): scaled = lax.all_gather(scaled, 'dp', axis=0, tiled=True)  102 us
    all_gather x1, waiting for transfers between devices, on_device(): scaled = lax.all_gather(scaled, 'flat', axis=1, tiled=True)  81.2 us
    reduce_scatter x1, waiting for transfers between devices, on_device(): lax.psum_scatter(shares, 'flat', scatter_dimension=1, tiled=True)  79.1 us
    psum x1, blocking collectives, on_device(): lax.psum(jnp.concatenate([local_values.reshape(kept // 128, 128), square]...  57.6 us
    pallas_call x1, Pallas kernels, sketch_pass(): pl.pallas_call(sketch_kernel, grid=(kept // tile,), out_shape=jax.ShapeDt...  49 us
    all_to_all x1, blocking collectives, on_device(): lax.all_to_all(activations, 'dp', split_axis=1, concat_axis=0, tiled=True)  48.8 us
    psum x1, blocking collectives, on_device(): lax.psum(jnp.sum(image * vector_now), ('flat', 'dp')).reshape(1)  33.5 us
  transfers between devices with their start and end apart: 4, of which 4 were waited for; matrix products, arithmetic and copies ran while one was open for 0% of the time, Pallas kernels for 0%

profile of v1, /device:TPU:0, one launch (start us, length us, event | category | flops | bytes accessed | tf_op | source)
XLA Modules:
  0.0 712.0 jit_solution(13398935606461971088)
XLA Ops:
  7.2 5.9 copy.17
  13.1 48.8 %all_to_all.19 = bf16[512,4,896]{0,2,1:T(8,128)(2,1)} all-to-all(bf16[512,4,896]{0,2,1:T(8,128)(2,1)} %bitcast.19), channel_id=1, replica_groups=mesh['groups'=2,'flat'=4,'dp'=4] {'dp'}, dimensions={1} | all-to-all | bytes 7340032 | tf_op jit(solution)/shard_map/all_to_all | solution.py:206
  61.9 6.0 copy.18
  67.9 25.9 %convolution_convert_fusion = bf16[2048,4096]{1,0:T(8,128)(2,1)} fusion(bf16[2048,896]{1,0:T(8,128)(2,1)} %bitcast.20, f32[896,4096]{1,0:T(8,128)} %v_ref.1), kind=kOutput, calls=%fused_computation | convolution fusion | flops 15044444160 | bytes 35127296 | tf_op jit(solution)/shard_map/dot_general | solution.py:207
  93.8 0.0 reduce-scatter.5.cloned.1.call-start
  93.9 127.4 %reduce-scatter.3.cloned.1.call-done = bf16[512,4096]{1,0:T(8,128)(2,1)} async-done(((bf16[2048,4096]{1,0:T(8,128)(2,1)}), bf16[512,4096]{1,0:T(8,128)(2,1)}) %reduce-scatter.3.cloned.1.call-update) | async-done | bytes 4194320 | tf_op jit(solution)/shard_map/reduce_scatter | solution.py:210
  221.3 79.1 %reduce-scatter.5.cloned.1.call-done = bf16[512,1024]{1,0:T(8,128)(2,1)} async-done(((bf16[512,4096]{1,0:T(8,128)(2,1)}), bf16[512,1024]{1,0:T(8,128)(2,1)}) %reduce-scatter.5.cloned.1.call-update) | async-done | bytes 1048592 | tf_op jit(solution)/shard_map/reduce_scatter | solution.py:211
  300.5 2.5 multiply_convert_fusion
  303.0 0.2 all-gather.5.cloned.1.call-start
  303.2 81.2 %all-gather.3.cloned.1.call-done = bf16[512,4096]{1,0:T(8,128)(2,1)} async-done(((bf16[512,1024]{1,0:T(8,128)(2,1)}), bf16[512,4096]{1,0:T(8,128)(2,1)}) %all-gather.3.cloned.1.call-update) | async-done | bytes 4194320 | tf_op jit(solution)/shard_map/all_gather | solution.py:213
  385.8 0.6 copy.20.row_ref
  386.4 2.0 copy.21.col_ref
  388.5 101.9 %all-gather.5.cloned.1.call-done = bf16[2048,4096]{1,0:T(8,128)(2,1)} async-done(((bf16[512,4096]{1,0:T(8,128)(2,1)}), bf16[2048,4096]{1,0:T(8,128)(2,1)}) %all-gather.5.cloned.1.call-update) | async-done | bytes 16777232 | tf_op jit(solution)/shard_map/all_gather | solution.py:214
  490.3 27.7 %multiply_reduce_fusion = (f32[]{:T(128)}, f32[896,4096]{1,0:T(8,128)}) fusion(f32[896,4096]{1,0:T(8,128)} %v_ref.1, f32[]{:T(128)} %bitcast.17, bf16[2048,4096]{1,0:T(8,128)(2,1)} %all-gather.5.cloned.1.call-done, bf16[2048,896]{1,0:T(8,128)(2,1)} %bitcast.21), kind=kOutput, calls=%fused_computation.2 | convolution fusion | flops 15047065600 | bytes 49807368 | tf_op jit(solution)/shard_map/dot_general | solution.py:215
  518.0 33.5 %psum.14 = f32[]{:T(128)} all-reduce(f32[]{:T(128)} %get-tuple-element.10), channel_id=1, replica_groups=mesh['groups'=2,'flat'=4,'dp'=4] {'flat','dp'}, use_global_device_ids=true, to_apply=%region_3.0 | all-reduce | flops 1 | bytes 8 | tf_op jit(solution)/shard_map/psum | solution.py:217
  552.1 0.1 pad_maximum_fusion.1.scalars
  552.2 25.5 %shard_map.120 = (f32[896,4096]{1,0:T(8,128)}, bf16[896,4096]{1,0:T(8,128)(2,1)S(1)}, f32[8,128]{1,0:T(8,128)S(1)}) custom-call(f32[2]{0:T(128)S(1)} %pad_maximum_fusion.1.scalars, f32[896,4096]{1,0:T(8,128)} %get-tuple-element.11.n_ref, f32[896,4096]{1,0:T(8,128)} %v_ref.1, f32[896,4096]{1,0:T(8,128)} %b_ref.1, s32[896,4096]{1,0:T(8,128)} %s_ref.1), custom_call_target="tpu_custom_call" | custom-call | tf_op jit(solution)/shard_map/pallas_call | solution.py:123
  577.8 49.0 %shard_map.121 = f32[4096,1]{1,0:T(8,128)S(1)} custom-call(s32[1]{0:T(128)} %bitcast.6.first_ref, bf16[896,4096]{1,0:T(8,128)(2,1)S(1)} %get-tuple-element.8.x_ref, s32[4096,1]{1,0:T(8,128)S(1)} %copy.20.row_ref, s32[4096,1]{1,0:T(8,128)S(1)} %copy-done), custom_call_target="tpu_custom_call" | custom-call | tf_op jit(solution)/shard_map/pallas_call | solution.py:175
  626.8 1.3 copy-done.1
  628.1 2.2 reduce
  630.4 57.6 %psum.15 = f32[40,128]{1,0:T(8,128)S(1)} all-reduce(f32[40,128]{1,0:T(8,128)S(1)} %pad_maximum_fusion), channel_id=1, replica_groups=mesh['groups'=2,'flat'=4,'dp'=4] {'flat','dp'}, use_global_device_ids=true, to_apply=%region_4.0 | all-reduce | flops 5120 | bytes 40960 | tf_op jit(solution)/shard_map/psum | solution.py:225
  688.0 0.6 slice_reduce_fusion
  689.3 0.6 fusion.1
  689.9 13.3 %broadcast_divide_fusion = f32[896,4096]{1,0:T(8,128)} fusion(f32[896,4096]{1,0:T(8,128)} %get-tuple-element.7, f32[]{:T(128)} %sqrt.3), kind=kLoop, calls=%fused_computation.3 | loop fusion | flops 3670016 | bytes 29360132 | tf_op jit(solution)/shard_map/div | solution.py:229
  (16 shorter events, 0.2 us)
Async XLA Ops:
  7.2 214.1 %reduce-scatter.3.cloned.1.call-start = ((), (), s32[]{:S(2)}) async-start(), calls=%async_computation.3 | async-start | bytes 20971520 | tf_op jit(solution)/shard_map/reduce_scatter | solution.py:210
  93.8 206.7 %copy-start.4 = (f32[512]{0:T(512)S(1)}, f32[512]{0:T(512)}, u32[]{:S(2)}) copy-start(f32[512]{0:T(512)} %param.10) | copy-start | bytes 6148
  93.8 291.9 %copy-start.2 = (s32[4096]{0:T(1024)S(1)}, s32[4096]{0:T(1024)}, u32[]{:S(2)}) copy-start(s32[4096]{0:T(1024)} %param.16) | copy-start | bytes 49156
  93.8 292.6 %copy-start.3 = (s32[4096]{0:T(1024)S(1)}, s32[4096]{0:T(1024)}, u32[]{:S(2)}) copy-start(s32[4096]{0:T(1024)} %param.17) | copy-start | bytes 49156
  93.8 206.6 %reduce-scatter.5.cloned.1.call-start = ((), (), s32[]{:S(2)}) async-start(), calls=%async_computation.4 | async-start | bytes 5242880 | tf_op jit(solution)/shard_map/reduce_scatter | solution.py:211
  221.3 163.1 %all-gather.3.cloned.1.call-start = ((), (), s32[]{:S(2)}) async-start(), calls=%async_computation.5 | async-start | bytes 5242880 | tf_op jit(solution)/shard_map/all_gather | solution.py:213
  303.0 187.3 %all-gather.5.cloned.1.call-start = ((), (), s32[]{:S(2)}) async-start(), calls=%async_computation.6 | async-start | bytes 20971520 | tf_op jit(solution)/shard_map/all_gather | solution.py:214
  552.2 25.5 %copy-start = (s32[4096,1]{1,0:T(8,128)S(1)}, s32[4096,1]{1,0:T(8,128)}, u32[]{:S(2)}) copy-start(s32[4096,1]{1,0:T(8,128)} %copy.21.col_ref) | copy-start | bytes 49156
  626.8 1.3 copy-start.1
Sparse Core Ops, SparseCore 0:
  94.0 127.2 reduce-scatter.2
  223.6 76.7 reduce-scatter.4
  303.1 81.2 all-gather.2
  385.8 104.4 all-gather.4

commit v2 on v1

--- a/solution.py
+++ b/solution.py
@@ -99,13 +99,16 @@
     return (vector_next, alpha_value.reshape(1), beta_value.reshape(1), sketch)
 
 
-def residual_kernel(scalars, n_ref, v_ref, b_ref, s_ref, r_ref, x_ref, sq_ref):
+def residual_kernel(scalars, v_ref, b_ref, s_ref, *refs):
+    n_refs, (r_ref, x_ref, sq_ref) = refs[:-3], refs[-3:]
+
     @pl.when(pl.program_id(0) == 0)
     def _():
         sq_ref[...] = jnp.zeros_like(sq_ref)
 
-    rows, width = n_ref.shape
-    residual = n_ref[...] - scalars[0] * v_ref[...] - scalars[1] * b_ref[...]
+    rows, width = v_ref.shape
+    image = jnp.concatenate([ref[...] for ref in n_refs], axis=1)
+    residual = image - scalars[0] * v_ref[...] - scalars[1] * b_ref[...]
     r_ref[...] = residual
     signs = (2 * s_ref[...] - 1).astype(jnp.float32)
     x_ref[...] = (signs * residual).astype(jnp.bfloat16)
@@ -116,9 +119,10 @@
     sq_ref[...] += total
 
 
-def residual_pass(scalars, image, vector_now, vector_before, sign_bits):
-    rows, width = image.shape
+def residual_pass(scalars, images, vector_now, vector_before, sign_bits):
+    rows, width = vector_now.shape
     tile = 64
+    narrow = pl.BlockSpec((tile, images[0].shape[1]), lambda i: (i, 0))
     block = pl.BlockSpec((tile, width), lambda i: (i, 0))
     return pl.pallas_call(
         residual_kernel,
@@ -128,10 +132,10 @@
             jax.ShapeDtypeStruct((rows, width), jnp.bfloat16),
             jax.ShapeDtypeStruct((8, 128), jnp.float32),
         ),
-        in_specs=[pl.BlockSpec(memory_space=pltpu.SMEM)] + [block] * 4,
+        in_specs=[pl.BlockSpec(memory_space=pltpu.SMEM)] + [block] * 3 + [narrow] * len(images),
         out_specs=(block, block, pl.BlockSpec((8, 128), lambda i: (0, 0))),
         compiler_params=pltpu.CompilerParams(vmem_limit_bytes=40 * 2**20),
-    )(scalars, image, vector_now, vector_before, sign_bits)
+    )(scalars, vector_now, vector_before, sign_bits, *images)
 
 
 def odd_bits(common):
@@ -202,21 +206,61 @@
     data_count = lax.axis_size("dp")
     rows, width = vector_now.shape
     total_cells = rows * width * flat_count * data_count
-    tokens = activations.shape[0] * data_count
-    columns = lax.all_to_all(activations, "dp", split_axis=1, concat_axis=0, tiled=True)
-    outputs = jnp.dot(
-        columns, vector_now.astype(jnp.bfloat16), preferred_element_type=jnp.float32
-    ).astype(jnp.bfloat16)
-    shares = lax.psum_scatter(outputs, "dp", scatter_dimension=0, tiled=True)
-    shares = lax.psum_scatter(shares, "flat", scatter_dimension=1, tiled=True).astype(jnp.float32)
-    scaled = (curvature[:, None] * shares / tokens).astype(jnp.bfloat16)
-    scaled = lax.all_gather(scaled, "flat", axis=1, tiled=True)
-    scaled = lax.all_gather(scaled, "dp", axis=0, tiled=True)
-    image = jnp.dot(columns.T, scaled, preferred_element_type=jnp.float32)
-    image = image + prior_precision[0] * vector_now
-    alpha_value = lax.psum(jnp.sum(image * vector_now), ("flat", "dp")).reshape(1) / total_cells
+    tok = activations.shape[0]
+    tokens = tok * data_count
+    part = tok // flat_count
+    place, own = lax.axis_index("flat"), lax.axis_index("dp")
+    levels = [1 << k for k in range(data_count.bit_length() - 1)]
+    masks = [0]
+    for mask in reversed(levels):
+        masks = masks + [mask ^ one for one in masks]
+
+    def swap(block, mask):
+        return lax.ppermute(block, "dp", [(i, i ^ mask) for i in range(data_count)])
+
+    def shift(block, by):
+        return lax.ppermute(block, "flat", [(i, (i + by) % flat_count) for i in range(flat_count)])
+
+    parts = activations.reshape(flat_count, part, -1)
+    back = parts[::-1]
+    turned = lax.dynamic_slice_in_dim(
+        jnp.concatenate([back, back]), flat_count - 1 - place, flat_count, 0
+    ).reshape(tok, -1)
+    weight = lax.dynamic_slice(curvature, (place * part,), (part,))[:, None]
+    pieces = []
+    for mask in masks:
+        piece = lax.dynamic_slice(turned, (0, (own ^ mask) * rows), (tok, rows))
+        pieces.append(swap(piece, mask) if mask else piece)
+    columns = jnp.concatenate(pieces, axis=0)
+    half = vector_now.astype(jnp.bfloat16)
+    chunk = width // 4
+    images = []
+    inner = jnp.float32(0)
+
+    def add(left, right):
+        return (left.astype(jnp.float32) + right.astype(jnp.float32)).astype(jnp.bfloat16)
+
+    for c in range(width // chunk):
+        cols = slice(c * chunk, (c + 1) * chunk)
+        held = jnp.dot(columns, half[:, cols], preferred_element_type=jnp.float32)
+        held = held.astype(jnp.bfloat16)
+        for mask in levels:
+            middle = held.shape[0] // 2
+            held = add(held[:middle], swap(held[middle:], mask))
+        total = held[:part].astype(jnp.float32)
+        for j in range(1, flat_count):
+            total = total + shift(held[j * part : (j + 1) * part], -j).astype(jnp.float32)
+        scaled = (weight * total / tokens).astype(jnp.bfloat16)
+        scaled = jnp.concatenate([scaled] + [shift(scaled, j) for j in range(1, flat_count)])
+        for mask in reversed(levels):
+            scaled = jnp.concatenate([scaled, swap(scaled, mask)])
+        image = jnp.dot(columns.T, scaled, preferred_element_type=jnp.float32)
+        image = image + prior_precision[0] * vector_now[:, cols]
+        inner = inner + jnp.sum(image * vector_now[:, cols])
+        images.append(image)
+    alpha_value = lax.psum(inner, ("flat", "dp")).reshape(1) / total_cells
     residual, signed, square = residual_pass(
-        jnp.concatenate([alpha_value, beta_before]), image, vector_now, vector_before, sign_bits
+        jnp.concatenate([alpha_value, beta_before]), images, vector_now, vector_before, sign_bits
     )
     own_index = lax.axis_index(("flat", "dp"))
     first_row = (own_index * (rows * width // (BLOCK * BLOCK))).reshape(1)

time: 713 us -> 688 us (0.965); the launches traced: 712 us -> 679 us
  waiting for transfers between devices: 390 us -> 257 us
  starting transfers between devices: 0.34 us -> 84 us
  blocking collectives: 140 us -> 87.8 us
  local copies, waits for them, and re-layouts: 15.9 us -> 54.6 us
  other arithmetic: 19.3 us -> 43.3 us
  matrix products: 53.6 us -> 69.1 us
  between operations: 18.7 us -> 9.04 us
    ppermute x0 -> x43, waiting for transfers between devices: none -> 257 us  [the longest x19 172 us: swap(): return lax.ppermute(block, 'dp', [(i, i ^ mask) for i in range(data_count)])]
    reduce_scatter x2 -> x0, waiting for transfers between devices: 206 us -> none  [the longest x1 127 us: on_device(): shares = lax.psum_scatter(outputs, 'dp', scatter_dimension=0, tiled=True)]
    all_gather x2 -> x0, waiting for transfers between devices: 183 us -> none  [the longest x1 102 us: on_device(): scaled = lax.all_gather(scaled, 'dp', axis=0, tiled=True)]
    ppermute x0 -> x43, starting transfers between devices: none -> 84 us  [the longest x24 70.3 us: shift(): lax.ppermute(block, 'flat', [(i, (i + by) % flat_count) for i in range(fl...]
    all_to_all x1 -> x0, blocking collectives: 48.8 us -> none  [on_device(): lax.all_to_all(activations, 'dp', split_axis=1, concat_axis=0, tiled=True)]
    unnamed x11 -> x74, local copies, waits for them, and re-layouts: 7.26 us -> 26.4 us
    convert_element_type x1 -> x9, other arithmetic: 2.5 us -> 18.2 us  [the longest x1 9.35 us: on_device(): half = vector_now.astype(jnp.bfloat16)]
    dot_general x1 -> x4, matrix products: 27.7 us -> 42.8 us  [on_device(): image = jnp.dot(columns.T, scaled, preferred_element_type=jnp.float32)]
  transfers between devices with their start and end apart: 4 -> 43, of which waited for: 4 -> 18; matrix products, arithmetic and copies ran while one was open for 0% -> 13% of each run, Pallas kernels for 0% -> 0%
where the time goes in v2:
time: 688 us; the launch traced here: 679 us
  waiting for transfers between devices  257 us (37%)
  blocking collectives  87.8 us (13%)
  starting transfers between devices  84 us (12%)
  Pallas kernels  74.9 us (11%)
  matrix products  69.1 us (10%)
  local copies, waits for them, and re-layouts  54.6 us (8%)
  other arithmetic  43.3 us (6%)
  between operations  9.04 us (1%)
    ppermute x19, waiting for transfers between devices, swap(): return lax.ppermute(block, 'dp', [(i, i ^ mask) for i in range(data_count)])  172 us
    ppermute x24, waiting for transfers between devices, shift(): lax.ppermute(block, 'flat', [(i, (i + by) % flat_count) for i in range(fl...  84.3 us
    ppermute x24, starting transfers between devices, shift(): lax.ppermute(block, 'flat', [(i, (i + by) % flat_count) for i in range(fl...  70.3 us
    psum x1, blocking collectives, on_device(): lax.psum(jnp.concatenate([local_values.reshape(kept // 128, 128), square]...  57.6 us
    pallas_call x1, Pallas kernels, sketch_pass(): pl.pallas_call(sketch_kernel, grid=(kept // tile,), out_shape=jax.ShapeDt...  49 us
    dot_general x4, matrix products, on_device(): image = jnp.dot(columns.T, scaled, preferred_element_type=jnp.float32)  42.8 us
    psum x1, blocking collectives, on_device(): alpha_value = lax.psum(inner, ('flat', 'dp')).reshape(1) / total_cells  30.2 us
    unnamed x74, local copies, waits for them, and re-layouts  26.4 us
  transfers between devices with their start and end apart: 43, of which 18 were waited for; matrix products, arithmetic and copies ran while one was open for 13% of the time, Pallas kernels for 0%

profile of v2, /device:TPU:0, one launch (start us, length us, event | category | flops | bytes accessed | tf_op | source)
XLA Modules:
  0.0 679.3 jit_solution(2844860224315378920)
XLA Ops:
  21.8 12.0 %collective-permute-done = bf16[512,896]{1,0:T(8,128)(2,1)} collective-permute-done((bf16[512,896]{1,0:T(8,128)(2,1)}, bf16[512,896]{1,0:T(8,128)(2,1)}, u32[]{:S(2)}, u32[]{:S(2)}) %collective-permute-start) | collective-permute-done | bytes 917536 | tf_op jit(solution)/shard_map/ppermute | solution.py:219
  33.8 18.0 %collective-permute-done.2 = bf16[512,896]{1,0:T(8,128)(2,1)} collective-permute-done((bf16[512,896]{1,0:T(8,128)(2,1)S(1)}, bf16[512,896]{1,0:T(8,128)(2,1)}, u32[]{:S(2)}, u32[]{:S(2)}) %collective-permute-start.2) | collective-permute-done | bytes 917536 | tf_op jit(solution)/shard_map/ppermute | solution.py:219
  96.0 16.8 %collective-permute-done.4 = bf16[512,1024]{1,0:T(8,128)(2,1)S(1)} collective-permute-done((bf16[512,1024]{1,0:T(8,128)(2,1)S(1)}, bf16[512,1024]{1,0:T(8,128)(2,1)S(1)}, u32[]{:S(2)}, u32[]{:S(2)}) %collective-permute-start.4) | collective-permute-done | bytes 1048608 | tf_op jit(solution)/shard_map/ppermute | solution.py:219
  117.1 18.1 %collective-permute-done.34 = bf16[512,1024]{1,0:T(8,128)(2,1)S(1)} collective-permute-done((bf16[512,1024]{1,0:T(8,128)(2,1)S(1)}, bf16[512,1024]{1,0:T(8,128)(2,1)S(1)}, u32[]{:S(2)}, u32[]{:S(2)}) %collective-permute-start.34) | collective-permute-done | bytes 1048608 | tf_op jit(solution)/shard_map/ppermute | solution.py:219
  137.4 20.2 %collective-permute-done.14 = bf16[512,1024]{1,0:T(8,128)(2,1)S(1)} collective-permute-done((bf16[512,1024]{1,0:T(8,128)(2,1)S(1)}, bf16[512,1024]{1,0:T(8,128)(2,1)S(1)}, u32[]{:S(2)}, u32[]{:S(2)}) %collective-permute-start.14) | collective-permute-done | bytes 1048608 | tf_op jit(solution)/shard_map/ppermute | solution.py:219
  162.7 17.0 %collective-permute-done.24 = bf16[512,1024]{1,0:T(8,128)(2,1)S(1)} collective-permute-done((bf16[512,1024]{1,0:T(8,128)(2,1)S(1)}, bf16[512,1024]{1,0:T(8,128)(2,1)S(1)}, u32[]{:S(2)}, u32[]{:S(2)}) %collective-permute-start.24) | collective-permute-done | bytes 1048608 | tf_op jit(solution)/shard_map/ppermute | solution.py:219
  190.0 12.5 %collective-permute-done.36 = bf16[128,1024]{1,0:T(8,128)(2,1)} collective-permute-done((bf16[128,1024]{1,0:T(8,128)(2,1)S(1)}, bf16[128,1024]{1,0:T(8,128)(2,1)}, u32[]{:S(2)}, u32[]{:S(2)}) %collective-permute-start.36) | collective-permute-done | bytes 262176 | tf_op jit(solution)/shard_map/ppermute | solution.py:222
  202.4 12.9 %collective-permute-start.26 = (bf16[128,1024]{1,0:T(8,128)(2,1)}, bf16[128,1024]{1,0:T(8,128)(2,1)}, u32[]{:S(2)}, u32[]{:S(2)}) collective-permute-start(bf16[128,1024]{1,0:T(8,128)(2,1)} %get-tuple-element.30), channel_id=1, source_target_pairs={{0,8},{4,12},{8,0},{12,4},{1,9},{5,13},{9,1},{13,5},{2,10},{6,14},... | collective-permute-start | bytes 786440 | tf_op jit(solution)/shard_map/ppermute | solution.py:222
  220.5 14.4 %collective-permute-done.16 = bf16[128,1024]{1,0:T(8,128)(2,1)} collective-permute-done((bf16[128,1024]{1,0:T(8,128)(2,1)}, bf16[128,1024]{1,0:T(8,128)(2,1)}, u32[]{:S(2)}, u32[]{:S(2)}) %collective-permute-start.16) | collective-permute-done | bytes 262176 | tf_op jit(solution)/shard_map/ppermute | solution.py:222
  260.7 10.5 %collective-permute-done.39 = bf16[128,1024]{1,0:T(8,128)(2,1)S(1)} collective-permute-done((bf16[128,1024]{1,0:T(8,128)(2,1)S(1)}, bf16[128,1024]{1,0:T(8,128)(2,1)S(1)}, u32[]{:S(2)}, u32[]{:S(2)}) %collective-permute-start.39) | collective-permute-done | bytes 262176 | tf_op jit(solution)/shard_map/ppermute | solution.py:222
  271.2 15.6 %collective-permute-start.18 = (bf16[128,1024]{1,0:T(8,128)(2,1)S(1)}, bf16[128,1024]{1,0:T(8,128)(2,1)S(1)}, u32[]{:S(2)}, u32[]{:S(2)}) collective-permute-start(bf16[128,1024]{1,0:T(8,128)(2,1)S(1)} %get-tuple-element.71), channel_id=1, source_target_pairs={{0,4},{4,8},{8,12},{12,0},{1,5},{5,9},{9,13},{13,1},{2,6},{6,10},{... | collective-permute-start | bytes 786440 | tf_op jit(solution)/shard_map/ppermute | solution.py:222
  291.0 11.8 %collective-permute-done.29 = bf16[128,1024]{1,0:T(8,128)(2,1)S(1)} collective-permute-done((bf16[128,1024]{1,0:T(8,128)(2,1)S(1)}, bf16[128,1024]{1,0:T(8,128)(2,1)S(1)}, u32[]{:S(2)}, u32[]{:S(2)}) %collective-permute-start.29) | collective-permute-done | bytes 262176 | tf_op jit(solution)/shard_map/ppermute | solution.py:222
  322.5 15.6 %collective-permute-done.41 = bf16[512,1024]{1,0:T(8,128)(2,1)S(1)} collective-permute-done((bf16[512,1024]{1,0:T(8,128)(2,1)S(1)}, bf16[512,1024]{1,0:T(8,128)(2,1)S(1)}, u32[]{:S(2)}, u32[]{:S(2)}) %collective-permute-start.41) | collective-permute-done | bytes 1048608 | tf_op jit(solution)/shard_map/ppermute | solution.py:219
  339.3 21.3 %collective-permute-done.31 = bf16[512,1024]{1,0:T(8,128)(2,1)S(1)} collective-permute-done((bf16[512,1024]{1,0:T(8,128)(2,1)S(1)}, bf16[512,1024]{1,0:T(8,128)(2,1)S(1)}, u32[]{:S(2)}, u32[]{:S(2)}) %collective-permute-start.31) | collective-permute-done | bytes 1048608 | tf_op jit(solution)/shard_map/ppermute | solution.py:219
  361.7 18.3 %collective-permute-done.21 = bf16[512,1024]{1,0:T(8,128)(2,1)S(1)} collective-permute-done((bf16[512,1024]{1,0:T(8,128)(2,1)S(1)}, bf16[512,1024]{1,0:T(8,128)(2,1)S(1)}, u32[]{:S(2)}, u32[]{:S(2)}) %collective-permute-start.21) | collective-permute-done | bytes 1048608 | tf_op jit(solution)/shard_map/ppermute | solution.py:219
  382.3 10.1 %collective-permute-done.8 = bf16[128,1024]{1,0:T(8,128)(2,1)S(1)} collective-permute-done((bf16[128,1024]{1,0:T(8,128)(2,1)S(1)}, bf16[128,1024]{1,0:T(8,128)(2,1)S(1)}, u32[]{:S(2)}, u32[]{:S(2)}) %collective-permute-start.8) | collective-permute-done | bytes 262176 | tf_op jit(solution)/shard_map/ppermute | solution.py:222
  413.5 14.9 %collective-permute-done.11 = bf16[512,1024]{1,0:T(8,128)(2,1)S(1)} collective-permute-done((bf16[512,1024]{1,0:T(8,128)(2,1)}, bf16[512,1024]{1,0:T(8,128)(2,1)S(1)}, u32[]{:S(2)}, u32[]{:S(2)}) %collective-permute-start.11) | collective-permute-done | bytes 1048608 | tf_op jit(solution)/shard_map/ppermute | solution.py:219
  446.9 10.2 %multiply_add_fusion.2.refs_1_ = f32[896,1024]{1,0:T(8,128)} fusion(f32[896,4096]{1,0:T(8,128)S(1)} %bitcast.20, f32[]{:T(128)} %bitcast.18, bf16[2048,1024]{1,0:T(8,128)(2,1)} %copy-done.20, bf16[512,896]{1,0:T(8,128)(2,1)} %collective-permute-done.2, bf16[512,896]{1,0:T(8,128)(2,1)} %collective-permute-done.1, bf16[512,896]{1,0:T(8,128)(2,1)} %collective-permute-done, ...), kind=kOutput, calls=%fused_computation.18 | convolution fusion | flops 3774611456 | bytes 15204356 | tf_op jit(solution)/shard_map/dot_general | solution.py:257
  465.3 17.4 %multiply_reduce_fusion = (f32[]{:T(128)}, f32[]{:T(128)}, f32[]{:T(128)}, f32[]{:T(128)}, f32[896,1024]{1,0:T(8,128)}) fusion(f32[896,4096]{1,0:T(8,128)} %v_ref.1, f32[896,1024]{1,0:T(8,128)} %multiply_add_fusion.3.refs_0_, f32[896,1024]{1,0:T(8,128)} %multiply_add_fusion.2.refs_1_, f32[896,1024]{1,0:T(8,128)S(1)} %multiply_add_fusion.1.refs_2_, ...), kind=kOutput, calls=%fused_computation.13 | convolution fusion | flops 3781951488 | bytes 37224468 | tf_op jit(solution)/shard_map/dot_general | solution.py:257
  485.2 30.2 %psum.14 = f32[]{:T(128)} all-reduce(f32[]{:T(128)S(6)} %add.142), channel_id=1, replica_groups=mesh['groups'=2,'flat'=4,'dp'=4] {'flat','dp'}, use_global_device_ids=true, to_apply=%region_4.0 | all-reduce | flops 1 | bytes 8 | tf_op jit(solution)/shard_map/psum | solution.py:261
  522.2 25.9 %shard_map.120 = (f32[896,4096]{1,0:T(8,128)}, bf16[896,4096]{1,0:T(8,128)(2,1)}, f32[8,128]{1,0:T(8,128)S(1)}) custom-call(f32[2]{0:T(128)S(1)} %pad_maximum_fusion.6.scalars, f32[896,4096]{1,0:T(8,128)} %v_ref.1, f32[896,4096]{1,0:T(8,128)} %b_ref.1, s32[896,4096]{1,0:T(8,128)} %s_ref.1, f32[896,1024]{1,0:T(8,128)S(1)} %copy-done.6, ...), custom_call_target="tpu_custom_call" | custom-call | tf_op jit(solution)/shard_map/pallas_call | solution.py:127
  551.2 49.0 %shard_map.121 = f32[4096,1]{1,0:T(8,128)S(1)} custom-call(s32[1]{0:T(128)} %bitcast.4.first_ref, bf16[896,4096]{1,0:T(8,128)(2,1)S(1)} %copy-done.2, s32[4096,1]{1,0:T(8,128)S(1)} %copy.13.row_ref, s32[4096,1]{1,0:T(8,128)S(1)} %copy-done), custom_call_target="tpu_custom_call" | custom-call | tf_op jit(solution)/shard_map/pallas_call | solution.py:179
  603.8 57.6 %psum.15 = f32[40,128]{1,0:T(8,128)S(1)} all-reduce(f32[40,128]{1,0:T(8,128)S(1)} %pad_maximum_fusion.5), channel_id=1, replica_groups=mesh['groups'=2,'flat'=4,'dp'=4] {'flat','dp'}, use_global_device_ids=true, to_apply=%region_5.0 | all-reduce | flops 5120 | bytes 40960 | tf_op jit(solution)/shard_map/psum | solution.py:269
  663.3 13.3 %broadcast_divide_fusion = f32[896,4096]{1,0:T(8,128)} fusion(f32[896,4096]{1,0:T(8,128)} %get-tuple-element.7, f32[]{:T(128)} %sqrt.3), kind=kLoop, calls=%fused_computation.2 | loop fusion | flops 3670016 | bytes 29360132 | tf_op jit(solution)/shard_map/div | solution.py:273
  (195 shorter events, 206.7 us)
Async XLA Ops:
  12.3 39.5 %collective-permute-start.2 = (bf16[512,896]{1,0:T(8,128)(2,1)S(1)}, bf16[512,896]{1,0:T(8,128)(2,1)}, u32[]{:S(2)}, u32[]{:S(2)}) collective-permute-start(bf16[512,896]{1,0:T(8,128)(2,1)S(1)} %get-tuple-element.23), channel_id=1, source_target_pairs={{0,3},{1,2},{2,1},{3,0},{4,7},{5,6},{6,5},{7,4},{8,11},{9,10},{10,... | collective-permute-start | bytes 2752520 | tf_op jit(solution)/shard_map/ppermute | solution.py:219
  91.1 44.0 %collective-permute-start.34 = (bf16[512,1024]{1,0:T(8,128)(2,1)S(1)}, bf16[512,1024]{1,0:T(8,128)(2,1)S(1)}, u32[]{:S(2)}, u32[]{:S(2)}) collective-permute-start(bf16[512,1024]{1,0:T(8,128)(2,1)S(1)} %slice.203), channel_id=1, source_target_pairs={{0,2},{1,3},{2,0},{3,1},{4,6},{5,7},{6,4},{7,5},{8,10},{9,11},{10,... | collective-permute-start | bytes 3145736 | tf_op jit(solution)/shard_map/ppermute | solution.py:219
  92.6 65.1 %collective-permute-start.14 = (bf16[512,1024]{1,0:T(8,128)(2,1)S(1)}, bf16[512,1024]{1,0:T(8,128)(2,1)S(1)}, u32[]{:S(2)}, u32[]{:S(2)}) collective-permute-start(bf16[512,1024]{1,0:T(8,128)(2,1)S(1)} %slice.185), channel_id=1, source_target_pairs={{0,2},{1,3},{2,0},{3,1},{4,6},{5,7},{6,4},{7,5},{8,10},{9,11},{10,... | collective-permute-start | bytes 3145736 | tf_op jit(solution)/shard_map/ppermute | solution.py:219
  95.6 84.1 %collective-permute-start.24 = (bf16[512,1024]{1,0:T(8,128)(2,1)S(1)}, bf16[512,1024]{1,0:T(8,128)(2,1)S(1)}, u32[]{:S(2)}, u32[]{:S(2)}) collective-permute-start(bf16[512,1024]{1,0:T(8,128)(2,1)S(1)} %slice.194), channel_id=1, source_target_pairs={{0,2},{1,3},{2,0},{3,1},{4,6},{5,7},{6,4},{7,5},{8,10},{9,11},{10,... | collective-permute-start | bytes 3145736 | tf_op jit(solution)/shard_map/ppermute | solution.py:219
  113.2 69.3 %collective-permute-start.5 = (bf16[128,1024]{1,0:T(8,128)(2,1)S(1)}, bf16[128,1024]{1,0:T(8,128)(2,1)S(1)}, u32[]{:S(2)}, u32[]{:S(2)}) collective-permute-start(bf16[128,1024]{1,0:T(8,128)(2,1)S(1)} %get-tuple-element.38), channel_id=1, source_target_pairs={{0,12},{4,0},{8,4},{12,8},{1,13},{5,1},{9,5},{13,9},{2,14},{6,2},{... | collective-permute-start | bytes 786440 | tf_op jit(solution)/shard_map/ppermute | solution.py:222
  117.0 67.1 %collective-permute-start.6 = (bf16[128,1024]{1,0:T(8,128)(2,1)S(1)}, bf16[128,1024]{1,0:T(8,128)(2,1)S(1)}, u32[]{:S(2)}, u32[]{:S(2)}) collective-permute-start(bf16[128,1024]{1,0:T(8,128)(2,1)S(1)} %get-tuple-element.40), channel_id=1, source_target_pairs={{0,8},{4,12},{8,0},{12,4},{1,9},{5,13},{9,1},{13,5},{2,10},{6,14},... | collective-permute-start | bytes 786440 | tf_op jit(solution)/shard_map/ppermute | solution.py:222
  135.2 53.5 %collective-permute-start.7 = (bf16[128,1024]{1,0:T(8,128)(2,1)S(1)}, bf16[128,1024]{1,0:T(8,128)(2,1)S(1)}, u32[]{:S(2)}, u32[]{:S(2)}) collective-permute-start(bf16[128,1024]{1,0:T(8,128)(2,1)S(1)} %get-tuple-element.39), channel_id=1, source_target_pairs={{0,4},{4,8},{8,12},{12,0},{1,5},{5,9},{9,13},{13,1},{2,6},{6,10},{... | collective-permute-start | bytes 786440 | tf_op jit(solution)/shard_map/ppermute | solution.py:222
  157.6 31.7 %collective-permute-start.35 = (bf16[128,1024]{1,0:T(8,128)(2,1)S(1)}, bf16[128,1024]{1,0:T(8,128)(2,1)}, u32[]{:S(2)}, u32[]{:S(2)}) collective-permute-start(bf16[128,1024]{1,0:T(8,128)(2,1)S(1)} %get-tuple-element.43), channel_id=1, source_target_pairs={{0,12},{4,0},{8,4},{12,8},{1,13},{5,1},{9,5},{13,9},{2,14},{6,2},{... | collective-permute-start | bytes 786440 | tf_op jit(solution)/shard_map/ppermute | solution.py:222
  184.1 31.2 %collective-permute-start.15 = (bf16[128,1024]{1,0:T(8,128)(2,1)S(1)}, bf16[128,1024]{1,0:T(8,128)(2,1)}, u32[]{:S(2)}, u32[]{:S(2)}) collective-permute-start(bf16[128,1024]{1,0:T(8,128)(2,1)S(1)} %get-tuple-element.33), channel_id=1, source_target_pairs={{0,12},{4,0},{8,4},{12,8},{1,13},{5,1},{9,5},{13,9},{2,14},{6,2},{... | collective-permute-start | bytes 786440 | tf_op jit(solution)/shard_map/ppermute | solution.py:222
  189.4 45.5 %collective-permute-start.16 = (bf16[128,1024]{1,0:T(8,128)(2,1)}, bf16[128,1024]{1,0:T(8,128)(2,1)}, u32[]{:S(2)}, u32[]{:S(2)}) collective-permute-start(bf16[128,1024]{1,0:T(8,128)(2,1)} %get-tuple-element.35), channel_id=1, source_target_pairs={{0,8},{4,12},{8,0},{12,4},{1,9},{5,13},{9,1},{13,5},{2,10},{6,14},... | collective-permute-start | bytes 786440 | tf_op jit(solution)/shard_map/ppermute | solution.py:222
  189.4 45.5 %collective-permute-start.17 = (bf16[128,1024]{1,0:T(8,128)(2,1)}, bf16[128,1024]{1,0:T(8,128)(2,1)}, u32[]{:S(2)}, u32[]{:S(2)}) collective-permute-start(bf16[128,1024]{1,0:T(8,128)(2,1)} %get-tuple-element.34), channel_id=1, source_target_pairs={{0,4},{4,8},{8,12},{12,0},{1,5},{5,9},{9,13},{13,1},{2,6},{6,10},{... | collective-permute-start | bytes 786440 | tf_op jit(solution)/shard_map/ppermute | solution.py:222
  202.4 32.5 %collective-permute-start.25 = (bf16[128,1024]{1,0:T(8,128)(2,1)}, bf16[128,1024]{1,0:T(8,128)(2,1)}, u32[]{:S(2)}, u32[]{:S(2)}) collective-permute-start(bf16[128,1024]{1,0:T(8,128)(2,1)} %get-tuple-element.28), channel_id=1, source_target_pairs={{0,12},{4,0},{8,4},{12,8},{1,13},{5,1},{9,5},{13,9},{2,14},{6,2},{... | collective-permute-start | bytes 786440 | tf_op jit(solution)/shard_map/ppermute | solution.py:222
  202.4 42.6 %collective-permute-start.26 = (bf16[128,1024]{1,0:T(8,128)(2,1)}, bf16[128,1024]{1,0:T(8,128)(2,1)}, u32[]{:S(2)}, u32[]{:S(2)}) collective-permute-start(bf16[128,1024]{1,0:T(8,128)(2,1)} %get-tuple-element.30), channel_id=1, source_target_pairs={{0,8},{4,12},{8,0},{12,4},{1,9},{5,13},{9,1},{13,5},{2,10},{6,14},... | collective-permute-start | bytes 786440 | tf_op jit(solution)/shard_map/ppermute | solution.py:222
  251.4 35.3 %collective-permute-start.40 = (bf16[128,1024]{1,0:T(8,128)(2,1)S(1)}, bf16[128,1024]{1,0:T(8,128)(2,1)S(1)}, u32[]{:S(2)}, u32[]{:S(2)}) collective-permute-start(bf16[128,1024]{1,0:T(8,128)(2,1)S(1)} %get-tuple-element.73), channel_id=1, source_target_pairs={{0,12},{4,0},{8,4},{12,8},{1,13},{5,1},{9,5},{13,9},{2,14},{6,2},{... | collective-permute-start | bytes 786440 | tf_op jit(solution)/shard_map/ppermute | solution.py:222
  254.3 35.8 %collective-permute-start.28 = (bf16[128,1024]{1,0:T(8,128)(2,1)S(1)}, bf16[128,1024]{1,0:T(8,128)(2,1)S(1)}, u32[]{:S(2)}, u32[]{:S(2)}) collective-permute-start(bf16[128,1024]{1,0:T(8,128)(2,1)S(1)} %get-tuple-element.15), channel_id=1, source_target_pairs={{0,4},{4,8},{8,12},{12,0},{1,5},{5,9},{9,13},{13,1},{2,6},{6,10},{... | collective-permute-start | bytes 786440 | tf_op jit(solution)/shard_map/ppermute | solution.py:222
  254.3 48.5 %collective-permute-start.29 = (bf16[128,1024]{1,0:T(8,128)(2,1)S(1)}, bf16[128,1024]{1,0:T(8,128)(2,1)S(1)}, u32[]{:S(2)}, u32[]{:S(2)}) collective-permute-start(bf16[128,1024]{1,0:T(8,128)(2,1)S(1)} %get-tuple-element.15), channel_id=1, source_target_pairs={{0,8},{4,12},{8,0},{12,4},{1,9},{5,13},{9,1},{13,5},{2,10},{6,14},... | collective-permute-start | bytes 786440 | tf_op jit(solution)/shard_map/ppermute | solution.py:222
  259.9 52.2 %collective-permute-start.30 = (bf16[128,1024]{1,0:T(8,128)(2,1)S(1)}, bf16[128,1024]{1,0:T(8,128)(2,1)S(1)}, u32[]{:S(2)}, u32[]{:S(2)}) collective-permute-start(bf16[128,1024]{1,0:T(8,128)(2,1)S(1)} %get-tuple-element.15), channel_id=1, source_target_pairs={{0,12},{4,0},{8,4},{12,8},{1,13},{5,1},{9,5},{13,9},{2,14},{6,2},{... | collective-permute-start | bytes 786440 | tf_op jit(solution)/shard_map/ppermute | solution.py:222
  271.2 42.5 %collective-permute-start.18 = (bf16[128,1024]{1,0:T(8,128)(2,1)S(1)}, bf16[128,1024]{1,0:T(8,128)(2,1)S(1)}, u32[]{:S(2)}, u32[]{:S(2)}) collective-permute-start(bf16[128,1024]{1,0:T(8,128)(2,1)S(1)} %get-tuple-element.71), channel_id=1, source_target_pairs={{0,4},{4,8},{8,12},{12,0},{1,5},{5,9},{9,13},{13,1},{2,6},{6,10},{... | collective-permute-start | bytes 786440 | tf_op jit(solution)/shard_map/ppermute | solution.py:222
  302.8 78.6 %collective-permute-start.10 = (bf16[128,1024]{1,0:T(8,128)(2,1)S(1)}, bf16[128,1024]{1,0:T(8,128)(2,1)S(1)}, u32[]{:S(2)}, u32[]{:S(2)}) collective-permute-start(bf16[128,1024]{1,0:T(8,128)(2,1)S(1)} %get-tuple-element.75), channel_id=1, source_target_pairs={{0,12},{4,0},{8,4},{12,8},{1,13},{5,1},{9,5},{13,9},{2,14},{6,2},{... | collective-permute-start | bytes 786440 | tf_op jit(solution)/shard_map/ppermute | solution.py:222
  313.6 47.0 %collective-permute-start.31 = (bf16[512,1024]{1,0:T(8,128)(2,1)S(1)}, bf16[512,1024]{1,0:T(8,128)(2,1)S(1)}, u32[]{:S(2)}, u32[]{:S(2)}) collective-permute-start(bf16[512,1024]{1,0:T(8,128)(2,1)S(1)} %pad_maximum_fusion.3), channel_id=1, source_target_pairs={{0,2},{1,3},{2,0},{3,1},{4,6},{5,7},{6,4},{7,5},{8,10},{9,11},{10,... | collective-permute-start | bytes 3145736 | tf_op jit(solution)/shard_map/ppermute | solution.py:219
  314.3 65.7 %collective-permute-start.21 = (bf16[512,1024]{1,0:T(8,128)(2,1)S(1)}, bf16[512,1024]{1,0:T(8,128)(2,1)S(1)}, u32[]{:S(2)}, u32[]{:S(2)}) collective-permute-start(bf16[512,1024]{1,0:T(8,128)(2,1)S(1)} %pad_maximum_fusion.2), channel_id=1, source_target_pairs={{0,2},{1,3},{2,0},{3,1},{4,6},{5,7},{6,4},{7,5},{8,10},{9,11},{10,... | collective-permute-start | bytes 3145736 | tf_op jit(solution)/shard_map/ppermute | solution.py:219
  339.3 90.7 %collective-permute-start.42 = (bf16[1024,1024]{1,0:T(8,128)(2,1)}, bf16[1024,1024]{1,0:T(8,128)(2,1)}, u32[]{:S(2)}, u32[]{:S(2)}) collective-permute-start(bf16[1024,1024]{1,0:T(8,128)(2,1)} %get-tuple-element.41), channel_id=1, source_target_pairs={{0,1},{1,0},{2,3},{3,2},{4,5},{5,4},{6,7},{7,6},{8,9},{9,8},{10,11... | collective-permute-start | bytes 6291464 | tf_op jit(solution)/shard_map/ppermute | solution.py:219
  361.7 70.5 %collective-permute-start.32 = (bf16[1024,1024]{1,0:T(8,128)(2,1)}, bf16[1024,1024]{1,0:T(8,128)(2,1)}, u32[]{:S(2)}, u32[]{:S(2)}) collective-permute-start(bf16[1024,1024]{1,0:T(8,128)(2,1)} %get-tuple-element.26), channel_id=1, source_target_pairs={{0,1},{1,0},{2,3},{3,2},{4,5},{5,4},{6,7},{7,6},{8,9},{9,8},{10,11... | collective-permute-start | bytes 6291464 | tf_op jit(solution)/shard_map/ppermute | solution.py:219
  381.2 54.3 %collective-permute-start.22 = (bf16[1024,1024]{1,0:T(8,128)(2,1)}, bf16[1024,1024]{1,0:T(8,128)(2,1)}, u32[]{:S(2)}, u32[]{:S(2)}) collective-permute-start(bf16[1024,1024]{1,0:T(8,128)(2,1)} %get-tuple-element.31), channel_id=1, source_target_pairs={{0,1},{1,0},{2,3},{3,2},{4,5},{5,4},{6,7},{7,6},{8,9},{9,8},{10,11... | collective-permute-start | bytes 6291464 | tf_op jit(solution)/shard_map/ppermute | solution.py:219
  (49 other events, 854.6 us)
